TPU v7x, 32 devices: a whole 2x2x4 slice. The times are simulated.
32 devices in a mesh: dp: 4 (over z), space: 8 (over y, x, core).
Axes of the slice: x: 2, y: 2, z: 4, core: 2. Of those that a mesh axis runs over, the one named last changes fastest.
Arguments:
- volume: bfloat16 [4, 8, 8, 64, 16, 256], P('dp', 'space'), may hold values from -6 to 6
- fine_filter: bfloat16 [3, 3, 3, 256, 256], P(None, None, None, 'dp'), may hold values from -0.078125 to 0.078125
- coarse_filter: bfloat16 [3, 3, 3, 256, 256], P(None, None, None, 'dp'), may hold values from -0.078125 to 0.078125
- fine_bias: float32 [256], replicated, may hold values from -3 to 3
- coarse_bias: float32 [256], replicated, may hold values from -3 to 3
Outputs:
- context: bfloat16 [4, 8, 8, 64, 16, 256], P('dp', 'space')
All inputs are finite; a program needn't handle non-finite values.
Results may differ from a plain program's by a relative error of at most 0.0047.
Values may be sent and summed in bfloat16 or wider, within the bound.
A program may use at most 192 MiB of HBM per device.

v0:
```python
import jax
import jax.numpy as jnp
from jax import lax
from jax.sharding import PartitionSpec as P

X = 64
BX = 8


def filters(shard):
    return lax.all_gather(shard, "dp", axis=3, tiled=True)


def dense_taps(grid, weights, bias):
    items, length_x, length_y, length_z, channels = grid.shape
    padded = jnp.pad(grid, ((0, 0), (1, 1), (1, 1), (1, 1), (0, 0)))
    total = jnp.zeros(grid.shape, jnp.float32)
    for step_x in range(3):
        for step_y in range(3):
            window = padded[:, step_x : step_x + length_x, step_y : step_y + length_y]
            stacked = jnp.concatenate(
                [window[:, :, :, depth : depth + length_z] for depth in range(3)], axis=-1
            )
            total = total + jnp.dot(
                stacked,
                weights[step_x, step_y].reshape(3 * channels, channels),
                preferred_element_type=jnp.float32,
            )
    return (grid.astype(jnp.float32) + jax.nn.gelu(total + bias)).astype(jnp.bfloat16)


def fine_cosets(brick):
    size_x, size_y, size_z, channels = brick.shape
    split = brick.reshape(size_x // 4, 4, size_y // 4, 4, size_z // 4, 4, channels)
    return split.transpose(1, 3, 5, 0, 2, 4, 6).reshape(
        64, size_x // 4, size_y // 4, size_z // 4, channels
    )


def fine_bricks(cosets):
    count, along_u, along_v, along_w, channels = cosets.shape
    split = cosets.reshape(4, 4, 4, along_u, along_v, along_w, channels).transpose(
        3, 0, 4, 1, 5, 2, 6
    )
    return split.reshape(along_u * 4, along_v * 4, along_w * 4, channels)


def assemble(parts):
    items, devices, along_u, along_v, along_w, channels = parts.shape
    across_x = X // BX
    across_y = devices // across_x
    grid = parts.reshape(items, across_x, across_y, along_u, along_v, along_w, channels).transpose(
        0, 1, 3, 2, 4, 5, 6
    )
    return grid.reshape(items, across_x * along_u, across_y * along_v, along_w, channels)


def disassemble(grid, along_u, along_v):
    items, size_x, size_y, along_w, channels = grid.shape
    across_x = size_x // along_u
    across_y = size_y // along_v
    parts = grid.reshape(items, across_x, along_u, across_y, along_v, along_w, channels).transpose(
        0, 1, 3, 2, 4, 5, 6
    )
    return parts.reshape(1, items, across_x * across_y, along_u, along_v, along_w, channels)


def split_halves(grid):
    items, size_x, size_y, size_z, channels = grid.shape
    parts = grid.reshape(items, size_x // 2, 2, size_y // 2, 2, size_z // 2, 2, channels).transpose(
        0, 2, 4, 6, 1, 3, 5, 7
    )
    return parts.reshape(items * 8, size_x // 2, size_y // 2, size_z // 2, channels)


def join_halves(parts, items):
    count, half_x, half_y, half_z, channels = parts.shape
    grid = parts.reshape(items, 2, 2, 2, half_x, half_y, half_z, channels).transpose(
        0, 4, 1, 5, 2, 6, 3, 7
    )
    return grid.reshape(items, half_x * 2, half_y * 2, half_z * 2, channels)


def on_device(volume, fine_filter, coarse_filter, fine_bias, coarse_bias):
    brick = volume[0, 0]
    devices = lax.axis_size("space")
    fine_weights = filters(fine_filter)
    coarse_weights = filters(coarse_filter)
    cosets = fine_cosets(brick)
    outgoing = cosets.reshape((devices, 64 // devices, 1) + cosets.shape[1:])
    received = lax.all_to_all(outgoing, "space", split_axis=0, concat_axis=2, tiled=True)
    items = received.shape[1]
    along_u = received.shape[3]
    along_v = received.shape[4]
    grid = dense_taps(assemble(received[0]), fine_weights, fine_bias)
    finer = dense_taps(split_halves(grid), coarse_weights, coarse_bias)
    grid = join_halves(finer, items)
    returned = lax.all_to_all(
        disassemble(grid, along_u, along_v), "space", split_axis=2, concat_axis=0, tiled=True
    )
    brick = fine_bricks(returned.reshape(cosets.shape))
    return brick.reshape(volume.shape)


def solution(mesh):
    return jax.shard_map(
        on_device,
        mesh=mesh,
        in_specs=(
            P("dp", "space", None, None, None, None),
            P(None, None, None, "dp", None),
            P(None, None, None, "dp", None),
            P(),
            P(),
        ),
        out_specs=P("dp", "space", None, None, None, None),
        check_vma=False,
    )
```

profile of v0, /device:TPU:3, one launch (start us, length us, event | category | flops | bytes accessed | tf_op | source)
XLA Modules:
  0.0 451.4 jit_solution(10222046831505784321)
XLA Ops:
  26.0 46.9 %all-to-all-done = bf16[8,8,1,2,16,4,256]{6,4,5,3,2,1,0:T(8,128)(2,1)} async-done(((bf16[8,8,1,2,16,4,256]{6,4,5,3,2,1,0:T(8,128)(2,1)}), bf16[8,8,1,2,16,4,256]{6,4,5,3,2,1,0:T(8,128)(2,1)}, u32[]{:S(2)}, u32[]{:S(2)}) %all-to-all-start) | async-done | bytes 4194336 | tf_op jit(solution)/shard_map/all_to_all | solution.py:91
  75.6 26.7 %pad_slice_fusion.28 = (bf16[8,16,16,4,256]{4,2,3,1,0:T(8,128)(2,1)}, bf16[8,16,16,4,256]{4,2,3,1,0:T(8,128)(2,1)}, bf16[8,16,16,4,256]{4,2,3,1,0:T(8,128)(2,1)}...) fusion(bf16[8,16,16,4,256]{4,2,3,1,0:T(8,128)(2,1)S(1)} %bitcas, ...), kind=kLoop, calls=%fused_computation.28 | loop fusion | bytes 83886080 | tf_op jit(solution)/shard_map/slice | solution.py:22
  102.3 10.2 %pad_slice_fusion.27 = (bf16[8,16,16,4,256]{4,2,3,1,0:T(8,128)(2,1)}, bf16[8,16,16,4,256]{4,2,3,1,0:T(8,128)(2,1)}, bf16[8,16,16,4,256]{4,2,3,1,0:T(8,128)(2,1)}...) fusion(bf16[8,16,16,4,256]{4,2,3,1,0:T(8,128)(2,1)S(1)} %bitcas, ...), kind=kLoop, calls=%fused_computation.27 | loop fusion | bytes 33554432 | tf_op jit(solution)/shard_map/slice | solution.py:22
  114.7 8.6 %fusion.24 = f32[8,16,16,4,256]{4,2,3,1,0:T(8,128)} fusion(bf16[768,256,1,1,1]{1,0,4,3,2:T(8,128)(2,1)S(1)} %bitcast.163, bf16[8,16,16,4,256]{4,2,3,1,0:T(8,128)(2,1)} %get-tuple-element.44, bf16[8,16,16,4,256]{4,2,3,1,0:T(8,128)(2,1)} %bitcast.135, bf16[8,16,16,4,256]{4,2,3,1,0:T(8,128)(2,1)} %get-tuple-element.43), kind=kOutput, calls=%fused_computation.76 | convolution fusion | flops 3258974208 | bytes 21364736 | tf_op jit(solution)/shard_map/dot_general | solution.py:24
  123.4 8.0 %fusion.6 = f32[8,16,16,4,256]{4,2,3,1,0:T(8,128)} fusion(bf16[768,256,1,1,1]{1,0,4,3,2:T(8,128)(2,1)S(1)} %bitcast.161, bf16[8,16,16,4,256]{4,2,3,1,0:T(8,128)(2,1)} %get-tuple-element.36, bf16[8,16,16,4,256]{4,2,3,1,0:T(8,128)(2,1)} %get-tuple-element.35, bf16[8,16,16,4,256]{4,2,3,1,0:T(8,128)(2,1)S(1)} %copy-done.12), kind=kOutput, calls=%fused_computation.58 | convolution fusion | flops 3258974208 | bytes 21364736 | tf_op jit(solution)/shard_map/dot_general | solution.py:24
  131.4 7.4 %fusion.12 = f32[8,16,16,4,256]{4,2,3,1,0:T(8,128)} fusion(bf16[768,256,1,1,1]{1,0,4,3,2:T(8,128)(2,1)S(1)} %bitcast.159, bf16[8,16,16,4,256]{4,2,3,1,0:T(8,128)(2,1)} %get-tuple-element.39, bf16[8,16,16,4,256]{4,2,3,1,0:T(8,128)(2,1)S(1)} %copy-done.11, bf16[8,16,16,4,256]{4,2,3,1,0:T(8,128)(2,1)S(1)} %copy-done.10), kind=kOutput, calls=%fused_computation.64 | convolution fusion | flops 3258974208 | bytes 21364736 | tf_op jit(solution)/shard_map/dot_general | solution.py:24
  138.8 8.0 %fusion.18 = f32[8,16,16,4,256]{4,2,3,1,0:T(8,128)} fusion(bf16[768,256,1,1,1]{1,0,4,3,2:T(8,128)(2,1)S(1)} %bitcast.157, bf16[8,16,16,4,256]{4,2,3,1,0:T(8,128)(2,1)} %get-tuple-element.42, bf16[8,16,16,4,256]{4,2,3,1,0:T(8,128)(2,1)} %get-tuple-element.41, bf16[8,16,16,4,256]{4,2,3,1,0:T(8,128)(2,1)S(1)} %copy-done.7), kind=kOutput, calls=%fused_computation.70 | convolution fusion | flops 3258974208 | bytes 21364736 | tf_op jit(solution)/shard_map/dot_general | solution.py:24
  146.8 7.5 %fusion.30 = f32[8,16,16,4,256]{4,2,3,1,0:T(8,128)} fusion(bf16[768,256,1,1,1]{1,0,4,3,2:T(8,128)(2,1)S(1)} %bitcast.155, bf16[8,16,16,4,256]{4,2,3,1,0:T(8,128)(2,1)} %get-tuple-element.47, bf16[8,16,16,4,256]{4,2,3,1,0:T(8,128)(2,1)S(1)} %copy-done.6, bf16[8,16,16,4,256]{4,2,3,1,0:T(8,128)(2,1)S(1)} %copy-done.5), kind=kOutput, calls=%fused_computation.82 | convolution fusion | flops 3258974208 | bytes 21364736 | tf_op jit(solution)/shard_map/dot_general | solution.py:24
  154.3 8.0 %fusion = f32[8,16,16,4,256]{4,2,3,1,0:T(8,128)} fusion(bf16[768,256,1,1,1]{1,0,4,3,2:T(8,128)(2,1)S(1)} %bitcast.153, bf16[8,16,16,4,256]{4,2,3,1,0:T(8,128)(2,1)} %get-tuple-element.33, bf16[8,16,16,4,256]{4,2,3,1,0:T(8,128)(2,1)S(1)} %copy-done.4, bf16[8,16,16,4,256]{4,2,3,1,0:T(8,128)(2,1)} %get-tuple-element.56), kind=kOutput, calls=%fused_computation.52 | convolution fusion | flops 3258974208 | bytes 21364736 | tf_op jit(solution)/shard_map/dot_general | solution.py:24
  162.3 7.3 %fusion.36 = f32[8,16,16,4,256]{4,2,3,1,0:T(8,128)} fusion(bf16[768,256,1,1,1]{1,0,4,3,2:T(8,128)(2,1)S(1)} %bitcast.151, bf16[8,16,16,4,256]{4,2,3,1,0:T(8,128)(2,1)} %get-tuple-element.51, bf16[8,16,16,4,256]{4,2,3,1,0:T(8,128)(2,1)S(1)} %copy-done.3, bf16[8,16,16,4,256]{4,2,3,1,0:T(8,128)(2,1)S(1)} %copy-done.2), kind=kOutput, calls=%fused_computation.88 | convolution fusion | flops 3258974208 | bytes 21364736 | tf_op jit(solution)/shard_map/dot_general | solution.py:24
  169.6 7.8 %fusion.42 = f32[8,16,16,4,256]{4,2,3,1,0:T(8,128)} fusion(bf16[768,256,1,1,1]{1,0,4,3,2:T(8,128)(2,1)S(1)} %bitcast.149, bf16[8,16,16,4,256]{4,2,3,1,0:T(8,128)(2,1)} %get-tuple-element.54, bf16[8,16,16,4,256]{4,2,3,1,0:T(8,128)(2,1)} %get-tuple-element.53, bf16[8,16,16,4,256]{4,2,3,1,0:T(8,128)(2,1)S(1)} %copy-done.17), kind=kOutput, calls=%fused_computation.94 | convolution fusion | flops 3258974208 | bytes 21364736 | tf_op jit(solution)/shard_map/dot_general | solution.py:24
  177.4 29.1 %fusion.116 = bf16[8,16,16,4,256]{4,2,3,1,0:T(8,128)(2,1)} fusion(f32[8,16,16,4,256]{4,2,3,1,0:T(8,128)} %fusion.42, f32[8,16,16,4,256]{4,2,3,1,0:T(8,128)} %fusion.36, f32[8,16,16,4,256]{4,2,3,1,0:T(8,128)} %fusion.30, f32[8,16,16,4,256]{4,2,3,1,0:T(8,128)} %fusion.24, f32[8,16,16,4,256]{4,2,3,1,0:T(8,128)} %fusion.18, ...), kind=kOutput, calls=%fused_computation.170 | convolution fusion | flops 3300917248 | bytes 88474624 | tf_op jit(solution)/shard_map/dot_general | solution.py:24
  218.6 9.8 %pad_slice_fusion.1 = (bf16[64,8,8,2,256]{4,2,3,1,0:T(8,128)(2,1)}, bf16[64,8,8,2,256]{4,2,3,1,0:T(8,128)(2,1)}, bf16[64,8,8,2,256]{4,2,3,1,0:T(8,128)(2,1)}, bf...) fusion(bf16[64,8,8,2,256]{4,2,3,1,0:T(8,128)(2,1)S(1)} %bitcast.137), kind=kLoop, calls=%fused_computation.1 | loop fusion | bytes 33554432 | tf_op jit(solution)/shard_map/slice | solution.py:22
  228.4 43.6 %pad_slice_fusion.2 = (bf16[64,8,8,2,256]{4,2,3,1,0:T(8,128)(2,1)}, bf16[64,8,8,2,256]{4,2,3,1,0:T(8,128)(2,1)}, bf16[64,8,8,2,256]{4,2,3,1,0:T(8,128)(2,1)}, bf...) fusion(bf16[64,8,8,2,256]{4,2,3,1,0:T(8,128)(2,1)} %bitcast.138), kind=kLoop, calls=%fused_computation.2 | loop fusion | bytes 83886080 | tf_op jit(solution)/shard_map/slice | solution.py:22
  275.4 8.4 %fusion.78 = f32[64,8,8,2,256]{4,2,3,1,0:T(8,128)} fusion(bf16[768,256,1,1,1]{1,0,4,3,2:T(8,128)(2,1)S(1)} %bitcast.164, bf16[64,8,8,2,256]{4,2,3,1,0:T(8,128)(2,1)} %get-tuple-element.18, bf16[64,8,8,2,256]{4,2,3,1,0:T(8,128)(2,1)} %bitcast.139, bf16[64,8,8,2,256]{4,2,3,1,0:T(8,128)(2,1)} %get-tuple-element.17), kind=kOutput, calls=%fused_computation.130 | convolution fusion | flops 3258974208 | bytes 21364736 | tf_op jit(solution)/shard_map/dot_general | solution.py:24
  283.9 8.9 %fusion.60 = f32[64,8,8,2,256]{4,2,3,1,0:T(8,128)} fusion(bf16[768,256,1,1,1]{1,0,4,3,2:T(8,128)(2,1)} %bitcast.162, bf16[64,8,8,2,256]{4,2,3,1,0:T(8,128)(2,1)} %get-tuple-element.10, bf16[64,8,8,2,256]{4,2,3,1,0:T(8,128)(2,1)} %get-tuple-element.9, bf16[64,8,8,2,256]{4,2,3,1,0:T(8,128)(2,1)} %get-tuple-element.8), kind=kOutput, calls=%fused_computation.112 | convolution fusion | flops 3258974208 | bytes 21364736 | tf_op jit(solution)/shard_map/dot_general | solution.py:24
  294.0 7.3 %fusion.54 = f32[64,8,8,2,256]{4,2,3,1,0:T(8,128)} fusion(bf16[768,256,1,1,1]{1,0,4,3,2:T(8,128)(2,1)} %bitcast.160, bf16[64,8,8,2,256]{4,2,3,1,0:T(8,128)(2,1)S(1)} %copy-done.16, bf16[64,8,8,2,256]{4,2,3,1,0:T(8,128)(2,1)S(1)} %copy-done.15, bf16[64,8,8,2,256]{4,2,3,1,0:T(8,128)(2,1)} %get-tuple-element.30), kind=kOutput, calls=%fused_computation.106 | convolution fusion | flops 3258974208 | bytes 21364736 | tf_op jit(solution)/shard_map/dot_general | solution.py:24
  301.3 8.9 %fusion.66 = f32[64,8,8,2,256]{4,2,3,1,0:T(8,128)} fusion(bf16[768,256,1,1,1]{1,0,4,3,2:T(8,128)(2,1)} %bitcast.158, bf16[64,8,8,2,256]{4,2,3,1,0:T(8,128)(2,1)} %get-tuple-element.13, bf16[64,8,8,2,256]{4,2,3,1,0:T(8,128)(2,1)} %get-tuple-element.12, bf16[64,8,8,2,256]{4,2,3,1,0:T(8,128)(2,1)} %get-tuple-element.11), kind=kOutput, calls=%fused_computation.118 | convolution fusion | flops 3258974208 | bytes 21364736 | tf_op jit(solution)/shard_map/dot_general | solution.py:24
  311.4 7.3 %fusion.72 = f32[64,8,8,2,256]{4,2,3,1,0:T(8,128)} fusion(bf16[768,256,1,1,1]{1,0,4,3,2:T(8,128)(2,1)} %bitcast.156, bf16[64,8,8,2,256]{4,2,3,1,0:T(8,128)(2,1)} %get-tuple-element.16, bf16[64,8,8,2,256]{4,2,3,1,0:T(8,128)(2,1)S(1)} %copy-done.14, bf16[64,8,8,2,256]{4,2,3,1,0:T(8,128)(2,1)S(1)} %copy-done.13), kind=kOutput, calls=%fused_computation.124 | convolution fusion | flops 3258974208 | bytes 21364736 | tf_op jit(solution)/shard_map/dot_general | solution.py:24
  318.7 9.1 %fusion.84 = f32[64,8,8,2,256]{4,2,3,1,0:T(8,128)} fusion(bf16[768,256,1,1,1]{1,0,4,3,2:T(8,128)(2,1)} %bitcast.154, bf16[64,8,8,2,256]{4,2,3,1,0:T(8,128)(2,1)} %get-tuple-element.21, bf16[64,8,8,2,256]{4,2,3,1,0:T(8,128)(2,1)} %get-tuple-element.20, bf16[64,8,8,2,256]{4,2,3,1,0:T(8,128)(2,1)} %get-tuple-element.19), kind=kOutput, calls=%fused_computation.136 | convolution fusion | flops 3258974208 | bytes 21364736 | tf_op jit(solution)/shard_map/dot_general | solution.py:24
  328.2 7.2 %fusion.90 = f32[64,8,8,2,256]{4,2,3,1,0:T(8,128)} fusion(bf16[768,256,1,1,1]{1,0,4,3,2:T(8,128)(2,1)S(1)} %bitcast.152, bf16[64,8,8,2,256]{4,2,3,1,0:T(8,128)(2,1)} %get-tuple-element.25, bf16[64,8,8,2,256]{4,2,3,1,0:T(8,128)(2,1)S(1)} %copy-done.9, bf16[64,8,8,2,256]{4,2,3,1,0:T(8,128)(2,1)S(1)} %copy-done.8), kind=kOutput, calls=%fused_computation.142 | convolution fusion | flops 3258974208 | bytes 21364736 | tf_op jit(solution)/shard_map/dot_general | solution.py:24
  335.4 8.5 %fusion.96 = f32[64,8,8,2,256]{4,2,3,1,0:T(8,128)} fusion(bf16[768,256,1,1,1]{1,0,4,3,2:T(8,128)(2,1)S(1)} %bitcast.150, bf16[64,8,8,2,256]{4,2,3,1,0:T(8,128)(2,1)} %get-tuple-element.28, bf16[64,8,8,2,256]{4,2,3,1,0:T(8,128)(2,1)} %get-tuple-element.27, bf16[64,8,8,2,256]{4,2,3,1,0:T(8,128)(2,1)} %get-tuple-element.26), kind=kOutput, calls=%fused_computation.148 | convolution fusion | flops 3258974208 | bytes 21364736 | tf_op jit(solution)/shard_map/dot_general | solution.py:24
  343.9 29.3 %fusion.125 = bf16[64,8,8,2,256]{4,2,3,1,0:T(8,128)(2,1)} fusion(f32[64,8,8,2,256]{4,2,3,1,0:T(8,128)} %fusion.96, f32[64,8,8,2,256]{4,2,3,1,0:T(8,128)} %fusion.90, f32[64,8,8,2,256]{4,2,3,1,0:T(8,128)} %fusion.84, f32[64,8,8,2,256]{4,2,3,1,0:T(8,128)} %fusion.78, f32[64,8,8,2,256]{4,2,3,1,0:T(8,128)} %fusion.72, f32[64,8,8,2,256]{4,2,3,1,0:T(8,128)} %fusion.66, ...), kind=kOutput, calls=%fused_computation.179 | convolution fusion | flops 3300917248 | bytes 88474624 | tf_op jit(solution)/shard_map/dot_general | solution.py:24
  379.5 51.7 %all_to_all.30 = bf16[1,8,8,2,16,4,256]{6,5,4,3,1,0,2:T(4,128)(2,1)S(1)} all-to-all(bf16[1,8,8,2,16,4,256]{6,5,4,3,1,0,2:T(4,128)(2,1)S(1)} %copy.21), channel_id=1, replica_groups=mesh['dp'=4,'space'=8] {'space'}, dimensions={2} | all-to-all | bytes 8388608 | tf_op jit(solution)/shard_map/all_to_all | solution.py:98
  (59 shorter events, 62.2 us)
Async XLA Ops:
  6.5 106.0 %all-gather.3.cloned.1.call-start = ((), (), s32[]{:S(2)}) async-start(), calls=%async_computation.2 | async-start | bytes 4423680 | tf_op jit(solution)/shard_map/all_gather | solution.py:11
  20.7 52.2 %all-to-all-start = ((bf16[8,8,1,2,16,4,256]{6,4,5,3,2,1,0:T(8,128)(2,1)}), bf16[8,8,1,2,16,4,256]{6,4,5,3,2,1,0:T(8,128)(2,1)}, u32[]{:S(2)}, u32[]{:S(2)}) async-start(bf16[8,8,1,2,16,4,256]{6,4,5,3,2,1,0:T(8,128)(2,1)} %bitcast.142), calls=%async_computation | async-start | bytes 8388608 | tf_op jit(solution)/shard_map/all_to_all | solution.py:91
  25.3 246.8 %all-gather.5.cloned.1.call-start = ((), (), s32[]{:S(2)}) async-start(), calls=%async_computation.3 | async-start | bytes 4423680 | tf_op jit(solution)/shard_map/all_gather | solution.py:11
  75.6 26.7 %copy-start = (bf16[1,8,8,1,2,16,4,256]{7,5,6,4,2,1,3,0:T(8,128)(2,1)}, bf16[1,8,8,1,2,16,4,256]{7,5,6,4,2,1,3,0:T(8,128)(2,1)S(1)}, u32[]{:S(2)}) copy-start(bf16[1,8,8,1,2,16,4,256]{7,5,6,4,2,1,3,0:T(8,128)(2,1)S(1)} %copy.18) | copy-start | bytes 12582916
  114.7 8.6 %copy-start.12 = (bf16[8,16,16,4,256]{4,2,3,1,0:T(8,128)(2,1)S(1)}, bf16[8,16,16,4,256]{4,2,3,1,0:T(8,128)(2,1)}, u32[]{:S(2)}) copy-start(bf16[8,16,16,4,256]{4,2,3,1,0:T(8,128)(2,1)} %get-tuple-element.34) | copy-start | bytes 12582916
  123.4 8.0 %copy-start.10 = (bf16[8,16,16,4,256]{4,2,3,1,0:T(8,128)(2,1)S(1)}, bf16[8,16,16,4,256]{4,2,3,1,0:T(8,128)(2,1)}, u32[]{:S(2)}) copy-start(bf16[8,16,16,4,256]{4,2,3,1,0:T(8,128)(2,1)} %get-tuple-element.37) | copy-start | bytes 12582916
  123.4 8.0 %copy-start.11 = (bf16[8,16,16,4,256]{4,2,3,1,0:T(8,128)(2,1)S(1)}, bf16[8,16,16,4,256]{4,2,3,1,0:T(8,128)(2,1)}, u32[]{:S(2)}) copy-start(bf16[8,16,16,4,256]{4,2,3,1,0:T(8,128)(2,1)} %get-tuple-element.38) | copy-start | bytes 12582916
  131.4 7.4 %copy-start.7 = (bf16[8,16,16,4,256]{4,2,3,1,0:T(8,128)(2,1)S(1)}, bf16[8,16,16,4,256]{4,2,3,1,0:T(8,128)(2,1)}, u32[]{:S(2)}) copy-start(bf16[8,16,16,4,256]{4,2,3,1,0:T(8,128)(2,1)} %get-tuple-element.40) | copy-start | bytes 12582916
  138.8 8.0 %copy-start.5 = (bf16[8,16,16,4,256]{4,2,3,1,0:T(8,128)(2,1)S(1)}, bf16[8,16,16,4,256]{4,2,3,1,0:T(8,128)(2,1)}, u32[]{:S(2)}) copy-start(bf16[8,16,16,4,256]{4,2,3,1,0:T(8,128)(2,1)} %get-tuple-element.45) | copy-start | bytes 12582916
  138.8 8.0 %copy-start.6 = (bf16[8,16,16,4,256]{4,2,3,1,0:T(8,128)(2,1)S(1)}, bf16[8,16,16,4,256]{4,2,3,1,0:T(8,128)(2,1)}, u32[]{:S(2)}) copy-start(bf16[8,16,16,4,256]{4,2,3,1,0:T(8,128)(2,1)} %get-tuple-element.46) | copy-start | bytes 12582916
  146.8 7.5 %copy-start.4 = (bf16[8,16,16,4,256]{4,2,3,1,0:T(8,128)(2,1)S(1)}, bf16[8,16,16,4,256]{4,2,3,1,0:T(8,128)(2,1)}, u32[]{:S(2)}) copy-start(bf16[8,16,16,4,256]{4,2,3,1,0:T(8,128)(2,1)} %get-tuple-element.32) | copy-start | bytes 12582916
  154.3 8.0 %copy-start.2 = (bf16[8,16,16,4,256]{4,2,3,1,0:T(8,128)(2,1)S(1)}, bf16[8,16,16,4,256]{4,2,3,1,0:T(8,128)(2,1)}, u32[]{:S(2)}) copy-start(bf16[8,16,16,4,256]{4,2,3,1,0:T(8,128)(2,1)} %get-tuple-element.48) | copy-start | bytes 12582916
  154.3 8.0 %copy-start.3 = (bf16[8,16,16,4,256]{4,2,3,1,0:T(8,128)(2,1)S(1)}, bf16[8,16,16,4,256]{4,2,3,1,0:T(8,128)(2,1)}, u32[]{:S(2)}) copy-start(bf16[8,16,16,4,256]{4,2,3,1,0:T(8,128)(2,1)} %get-tuple-element.49) | copy-start | bytes 12582916
  162.3 7.3 %copy-start.17 = (bf16[8,16,16,4,256]{4,2,3,1,0:T(8,128)(2,1)S(1)}, bf16[8,16,16,4,256]{4,2,3,1,0:T(8,128)(2,1)}, u32[]{:S(2)}) copy-start(bf16[8,16,16,4,256]{4,2,3,1,0:T(8,128)(2,1)} %get-tuple-element.52) | copy-start | bytes 12582916
  169.6 7.8 %copy-start.18 = (f32[256]{0:T(256)S(1)}, f32[256]{0:T(256)}, u32[]{:S(2)}) copy-start(f32[256]{0:T(256)} %param.8) | copy-start | bytes 3076
  216.7 2.0 copy-start.1
  283.9 8.9 %copy-start.15 = (bf16[64,8,8,2,256]{4,2,3,1,0:T(8,128)(2,1)S(1)}, bf16[64,8,8,2,256]{4,2,3,1,0:T(8,128)(2,1)}, u32[]{:S(2)}) copy-start(bf16[64,8,8,2,256]{4,2,3,1,0:T(8,128)(2,1)} %get-tuple-element.6) | copy-start | bytes 12582916
  283.9 10.1 %copy-start.16 = (bf16[64,8,8,2,256]{4,2,3,1,0:T(8,128)(2,1)S(1)}, bf16[64,8,8,2,256]{4,2,3,1,0:T(8,128)(2,1)}, u32[]{:S(2)}) copy-start(bf16[64,8,8,2,256]{4,2,3,1,0:T(8,128)(2,1)} %get-tuple-element.7) | copy-start | bytes 12582916
  301.3 8.9 %copy-start.13 = (bf16[64,8,8,2,256]{4,2,3,1,0:T(8,128)(2,1)S(1)}, bf16[64,8,8,2,256]{4,2,3,1,0:T(8,128)(2,1)}, u32[]{:S(2)}) copy-start(bf16[64,8,8,2,256]{4,2,3,1,0:T(8,128)(2,1)} %get-tuple-element.14) | copy-start | bytes 12582916
  301.3 10.1 %copy-start.14 = (bf16[64,8,8,2,256]{4,2,3,1,0:T(8,128)(2,1)S(1)}, bf16[64,8,8,2,256]{4,2,3,1,0:T(8,128)(2,1)}, u32[]{:S(2)}) copy-start(bf16[64,8,8,2,256]{4,2,3,1,0:T(8,128)(2,1)} %get-tuple-element.15) | copy-start | bytes 12582916
  318.7 9.1 %copy-start.8 = (bf16[64,8,8,2,256]{4,2,3,1,0:T(8,128)(2,1)S(1)}, bf16[64,8,8,2,256]{4,2,3,1,0:T(8,128)(2,1)}, u32[]{:S(2)}) copy-start(bf16[64,8,8,2,256]{4,2,3,1,0:T(8,128)(2,1)} %get-tuple-element.22) | copy-start | bytes 12582916
  318.7 9.5 %copy-start.9 = (bf16[64,8,8,2,256]{4,2,3,1,0:T(8,128)(2,1)S(1)}, bf16[64,8,8,2,256]{4,2,3,1,0:T(8,128)(2,1)}, u32[]{:S(2)}) copy-start(bf16[64,8,8,2,256]{4,2,3,1,0:T(8,128)(2,1)} %get-tuple-element.23) | copy-start | bytes 12582916
  335.4 8.5 %copy-start.19 = (f32[256]{0:T(256)S(1)}, f32[256]{0:T(256)}, u32[]{:S(2)}) copy-start(f32[256]{0:T(256)} %param.9) | copy-start | bytes 3076
Sparse Core Ops, SparseCore 0:
  8.9 71.1 all-gather.2
  81.7 68.5 all-gather.4
where the time goes:
time: 458 us; the launch traced here: 451 us
  matrix products  187 us (41%)
  local copies, waits for them, and re-layouts  146 us (32%)
  blocking collectives  51.7 us (11%)
  waiting for transfers between devices  48.3 us (11%)
  between operations  13.7 us (3%)
    dot_general x18, matrix products, dense_taps(): jnp.dot(stacked, weights[step_x, step_y].reshape(3 * channels, channels),...  187 us
    slice x4, local copies, waits for them, and re-layouts, dense_taps(): window[:, :, :, depth:depth + length_z]  90.3 us
    all_to_all x1, blocking collectives, on_device(): lax.all_to_all(disassemble(grid, along_u, along_v), 'space', split_axis=2...  51.7 us
    all_to_all x1, waiting for transfers between devices, on_device(): lax.all_to_all(outgoing, 'space', split_axis=0, concat_axis=2, tiled=True)  46.9 us
  transfers between devices with their start and end apart: 3, of which 1 were waited for; matrix products, arithmetic and copies ran while one was open for 47% of the time, Pallas kernels for 0%

commit v1 on v0

--- a/solution.py
+++ b/solution.py
@@ -1,6 +1,8 @@
 import jax
 import jax.numpy as jnp
 from jax import lax
+from jax.experimental import pallas as pl
+from jax.experimental.pallas import tpu as pltpu
 from jax.sharding import PartitionSpec as P
 
 X = 64
@@ -81,9 +83,224 @@
     return grid.reshape(items, half_x * 2, half_y * 2, half_z * 2, channels)
 
 
+MESH = pl.DeviceIdType.MESH
+N = 8
+S = 16
+F32 = jnp.float32
+
+
+def place(owner, k):
+    number = 2 * owner + k
+    return lax.div(number, 4), lax.rem(number, 4)
+
+
+def spread(rows, shift):
+    zero = jnp.zeros((S, shift, rows.shape[-1]), F32)
+    before = jnp.concatenate([zero, rows[:, : S - shift]], axis=1)
+    after = jnp.concatenate([rows[:, shift:], zero], axis=1)
+    return before.astype(jnp.bfloat16), after.astype(jnp.bfloat16)
+
+
+def taps(grid, x, step, weights):
+    acc = None
+    for dx in range(3):
+        for dy in range(3):
+            lhs = grid[x + dx * step, pl.ds(dy * step, S)].reshape(S * S, 768)
+            part = jnp.dot(lhs, weights[3 * dx + dy], preferred_element_type=F32)
+            acc = part if acc is None else acc + part
+    return acc
+
+
+def fill(grid, x, pad, rows, shift):
+    before, after = spread(rows.astype(F32), shift)
+    grid[x, pl.ds(pad, S), :, 0:256] = before
+    grid[x, pl.ds(pad, S), :, 256:512] = rows
+    grid[x, pl.ds(pad, S), :, 512:768] = after
+
+
+def clear(grid, pad):
+    side = S + 2 * pad
+    for edge in list(range(pad)) + list(range(S + pad, side)):
+        grid[edge] = jnp.zeros((side, S, 768), jnp.bfloat16)
+
+    @pl.loop(pad, S + pad)
+    def _(x):
+        grid[x, 0:pad] = jnp.zeros((pad, S, 768), jnp.bfloat16)
+        grid[x, S + pad : side] = jnp.zeros((pad, S, 768), jnp.bfloat16)
+
+
+def kernel(
+    vol, fw, cw, fb, cb, out, recv, fine, coarse, done,
+    in_send, in_recv, in_own, out_send, out_recv, out_own,
+):
+    me = lax.axis_index("space")
+
+    barrier = pltpu.get_barrier_semaphore()
+    for s in range(1, N):
+        pl.semaphore_signal(
+            barrier, inc=1, device_id={"space": lax.rem(me + s, N)}, device_id_type=MESH
+        )
+    pl.semaphore_wait(barrier, N - 1)
+
+    def incoming(k, s):
+        peer = lax.rem(me + s, N)
+        cx, cy = place(peer, k)
+        return pltpu.make_async_remote_copy(
+            src_ref=vol.at[:, cx, :, cy],
+            dst_ref=recv.at[k, pl.ds(2 * me, 2)],
+            send_sem=in_send.at[k, s],
+            recv_sem=in_recv.at[k, s],
+            device_id={"space": peer},
+            device_id_type=MESH,
+        )
+
+    def incoming_own(k):
+        cx, cy = place(me, k)
+        return pltpu.make_async_copy(
+            vol.at[:, cx, :, cy], recv.at[k, pl.ds(2 * me, 2)], in_own.at[k]
+        )
+
+    def outgoing(k, s):
+        peer = lax.rem(me + s, N)
+        cx, cy = place(me, k)
+        return pltpu.make_async_remote_copy(
+            src_ref=done.at[k, pl.ds(2 * peer, 2)],
+            dst_ref=out.at[:, cx, :, cy],
+            send_sem=out_send.at[k, s],
+            recv_sem=out_recv.at[k, s],
+            device_id={"space": peer},
+            device_id_type=MESH,
+        )
+
+    def outgoing_own(k):
+        cx, cy = place(me, k)
+        return pltpu.make_async_copy(
+            done.at[k, pl.ds(2 * me, 2)], out.at[:, cx, :, cy], out_own.at[k]
+        )
+
+    def arrival(k, s):
+        owner = lax.rem(me + N - s, N)
+        cx, cy = place(owner, k)
+        return pltpu.make_async_remote_copy(
+            src_ref=done.at[k, pl.ds(2 * me, 2)],
+            dst_ref=out.at[:, cx, :, cy],
+            send_sem=out_send.at[k, s],
+            recv_sem=out_recv.at[k, s],
+            device_id={"space": lax.rem(me + s, N)},
+            device_id_type=MESH,
+        )
+
+    def landing(k, s):
+        owner = lax.rem(me + N - s, N)
+        cx, cy = place(me, k)
+        return pltpu.make_async_remote_copy(
+            src_ref=vol.at[:, cx, :, cy],
+            dst_ref=recv.at[k, pl.ds(2 * owner, 2)],
+            send_sem=in_send.at[k, s],
+            recv_sem=in_recv.at[k, s],
+            device_id={"space": lax.rem(me + s, N)},
+            device_id_type=MESH,
+        )
+
+    for k in range(2):
+        incoming_own(k).start()
+
+        @pl.loop(1, N)
+        def _(s):
+            incoming(k, s).start()
+
+    clear(fine, 1)
+    clear(coarse, 2)
+
+    @pl.loop(0, 2)
+    def _(k):
+        def take(owner):
+            for i in range(2):
+                x = 2 * owner + i
+                fill(fine, x + 1, 1, recv[k, x], 4)
+
+        incoming_own(k).wait()
+        take(me)
+
+        @pl.loop(1, N)
+        def _(s):
+            landing(k, s).wait_recv()
+            take(lax.rem(me + N - s, N))
+
+        @pl.loop(0, S)
+        def _(x):
+            total = taps(fine, x, 1, fw)
+            own = fine[x + 1, pl.ds(1, S), :, 256:512].reshape(S * S, 256)
+            middle = own.astype(F32) + jax.nn.gelu(total + fb[...])
+            fill(coarse, x + 2, 2, middle.astype(jnp.bfloat16).reshape(S, S, 256), 8)
+
+        def finish(x):
+            total = taps(coarse, x, 2, cw)
+            own = coarse[x + 2, pl.ds(2, S), :, 256:512].reshape(S * S, 256)
+            result = own.astype(F32) + jax.nn.gelu(total + cb[...])
+            done[k, x] = result.astype(jnp.bfloat16).reshape(S, S, 256)
+
+        @pl.loop(1, N)
+        def _(s):
+            peer = lax.rem(me + s, N)
+
+            @pl.loop(0, 2)
+            def _(i):
+                finish(2 * peer + i)
+
+            outgoing(k, s).start()
+
+        @pl.loop(0, 2)
+        def _(i):
+            finish(2 * me + i)
+
+        outgoing_own(k).start()
+
+    for k in range(2):
+        outgoing_own(k).wait()
+
+        @pl.loop(1, N)
+        def _(s):
+            incoming(k, s).wait_send()
+            outgoing(k, s).wait_send()
+            arrival(k, s).wait_recv()
+
+
+def fused(volume, fine_filter, coarse_filter, fine_bias, coarse_bias):
+    bf16 = jnp.bfloat16
+    fw = filters(fine_filter).reshape(9, 768, 256)
+    cw = filters(coarse_filter).reshape(9, 768, 256)
+    vmem = pl.BlockSpec(memory_space=pltpu.VMEM)
+    hbm = pl.BlockSpec(memory_space=pl.ANY)
+    dma = pltpu.SemaphoreType.DMA
+    result = pl.pallas_call(
+        kernel,
+        out_shape=jax.ShapeDtypeStruct((2, 4, S, 4, S, 256), bf16),
+        in_specs=[hbm, vmem, vmem, vmem, vmem],
+        out_specs=hbm,
+        scratch_shapes=[
+            pltpu.VMEM((2, S, S, S, 256), bf16),
+            pltpu.VMEM((S + 2, S + 2, S, 768), bf16),
+            pltpu.VMEM((S + 4, S + 4, S, 768), bf16),
+            pltpu.VMEM((2, S, S, S, 256), bf16),
+            dma((2, N)), dma((2, N)), dma((2,)),
+            dma((2, N)), dma((2, N)), dma((2,)),
+        ],
+        compiler_params=pltpu.CompilerParams(
+            collective_id=0, has_side_effects=True, vmem_limit_bytes=56 * 2**20
+        ),
+    )(
+        volume.reshape(2, 4, S, 4, S, 256), fw, cw,
+        fine_bias.reshape(1, 256), coarse_bias.reshape(1, 256),
+    )
+    return result.reshape(volume.shape)
+
+
 def on_device(volume, fine_filter, coarse_filter, fine_bias, coarse_bias):
+    devices = lax.axis_size("space")
+    if devices == N and volume.shape == (1, 1, 8, 64, 16, 256):
+        return fused(volume, fine_filter, coarse_filter, fine_bias, coarse_bias)
     brick = volume[0, 0]
-    devices = lax.axis_size("space")
     fine_weights = filters(fine_filter)
     coarse_weights = filters(coarse_filter)
     cosets = fine_cosets(brick)

time: 458 us -> 277 us (0.60); the launches traced: 451 us -> 277 us
  matrix products: 187 us -> 0 us
  local copies, waits for them, and re-layouts: 146 us -> 4.47 us
  Pallas kernels: 0 us -> 116 us
  waiting for transfers between devices: 48.3 us -> 144 us
  blocking collectives: 51.7 us -> 0 us
    dot_general x18 -> x0, matrix products: 187 us -> none  [dense_taps(): jnp.dot(stacked, weights[step_x, step_y].reshape(3 * channels, channels),...]
    all_gather x2, waiting for transfers between devices: 0.02 us -> 142 us  [filters(): return lax.all_gather(shard, 'dp', axis=3, tiled=True)]
    pallas_call x0 -> x1, Pallas kernels: none -> 116 us  [fused(): pl.pallas_call(kernel, out_shape=jax.ShapeDtypeStruct((2, 4, S, 4, S, 256...]
    slice x6 -> x0, local copies, waits for them, and re-layouts: 95.9 us -> none  [the longest x4 90.3 us: dense_taps(): window[:, :, :, depth:depth + length_z]]
    all_to_all x1 -> x0, blocking collectives: 51.7 us -> none  [on_device(): lax.all_to_all(disassemble(grid, along_u, along_v), 'space', split_axis=2...]
    all_to_all x1 -> x0, waiting for transfers between devices: 46.9 us -> none  [on_device(): lax.all_to_all(outgoing, 'space', split_axis=0, concat_axis=2, tiled=True)]
    another operation x3 -> x0, local copies, waits for them, and re-layouts: 16.2 us -> none  [the longest x1 6.89 us: fine_cosets(): brick.reshape(size_x // 4, 4, size_y // 4, 4, size_z // 4, 4, channels)]
    transpose x3 -> x0, local copies, waits for them, and re-layouts: 14.8 us -> none  [the longest x1 6.59 us: fine_cosets(): split.transpose(1, 3, 5, 0, 2, 4, 6)]
  transfers between devices with their start and end apart: 3 -> 2, of which waited for: 1 -> 2; matrix products, arithmetic and copies ran while one was open for 47% -> 0% of each run, Pallas kernels for 0% -> 0%
where the time goes in v1:
time: 277 us
  waiting for transfers between devices  144 us (52%)
  Pallas kernels  116 us (42%)
  between operations  13.4 us (5%)
  local copies, waits for them, and re-layouts  4.47 us (2%)
    all_gather x2, waiting for transfers between devices, filters(): return lax.all_gather(shard, 'dp', axis=3, tiled=True)  142 us
    pallas_call x1, Pallas kernels, fused(): pl.pallas_call(kernel, out_shape=jax.ShapeDtypeStruct((2, 4, S, 4, S, 256...  116 us
  transfers between devices with their start and end apart: 2, of which 2 were waited for; matrix products, arithmetic and copies ran while one was open for 0% of the time, Pallas kernels for 0%

profile of v1, /device:TPU:3, one launch (start us, length us, event | category | flops | bytes accessed | tf_op | source)
XLA Modules:
  0.0 277.3 jit_solution(13019009296807500154)
XLA Ops:
  6.5 0.0 all-gather.3.cloned.1.call-start
  6.5 0.7 all-gather.3.cloned.1.call-update
  7.3 0.0 all-gather.5.cloned.1.call-start
  7.3 0.7 all-gather.5.cloned.1.call-update
  8.0 72.1 %all-gather.3.cloned.1.call-done = bf16[3,3,3,256,256]{4,3,2,1,0:T(8,128)(2,1)} async-done(((bf16[3,3,3,64,256]{4,3,2,1,0:T(8,128)(2,1)}), bf16[3,3,3,256,256]{4,3,2,1,0:T(8,128)(2,1)}) %all-gather.3.cloned.1.call-update) | async-done | bytes 3538960 | tf_op jit(solution)/shard_map/all_gather | solution.py:13
  80.1 70.2 %all-gather.5.cloned.1.call-done = bf16[3,3,3,256,256]{4,3,2,1,0:T(8,128)(2,1)} async-done(((bf16[3,3,3,64,256]{4,3,2,1,0:T(8,128)(2,1)}), bf16[3,3,3,256,256]{4,3,2,1,0:T(8,128)(2,1)}) %all-gather.5.cloned.1.call-update) | async-done | bytes 3538960 | tf_op jit(solution)/shard_map/all_gather | solution.py:13
  150.3 115.6 %shard_map.55 = bf16[2,4,16,4,16,256]{5,4,3,2,1,0:T(8,128)(2,1)} custom-call(bf16[2,4,16,4,16,256]{5,4,3,2,1,0:T(8,128)(2,1)} %bitcast.7, bf16[9,768,256]{2,1,0:T(8,128)(2,1)} %bitcast.8, bf16[9,768,256]{2,1,0:T(8,128)(2,1)} %bitcast.9, f32[1,256]{1,0:T(1,128)} %bitcast.10, f32[1,256]{1,0:T(1,128)} %bitcast.11), custom_call_target="tpu_custom_call" | custom-call | tf_op jit(solution)/shard_map/pallas_call | solution.py:276
  266.0 4.5 %copy.7 = bf16[1,1,8,64,16,256]{5,4,3,2,1,0:T(8,128)(2,1)} copy(bf16[1,1,8,64,16,256]{5,4,3,2,1,0:T(8,128)(2,1)} %bitcast.6) | data formatting | bytes 8388608
Async XLA Ops:
  6.5 73.6 %all-gather.3.cloned.1.call-start = ((), (), s32[]{:S(2)}) async-start(), calls=%async_computation | async-start | bytes 4423680 | tf_op jit(solution)/shard_map/all_gather | solution.py:13
  7.3 143.1 %all-gather.5.cloned.1.call-start = ((), (), s32[]{:S(2)}) async-start(), calls=%async_computation.1 | async-start | bytes 4423680 | tf_op jit(solution)/shard_map/all_gather | solution.py:13
Sparse Core Ops, SparseCore 0:
  8.9 71.1 all-gather.2
  81.7 68.5 all-gather.4

commit v2 on v1

--- a/solution.py
+++ b/solution.py
@@ -106,7 +106,8 @@
     for dx in range(3):
         for dy in range(3):
             lhs = grid[x + dx * step, pl.ds(dy * step, S)].reshape(S * S, 768)
-            part = jnp.dot(lhs, weights[3 * dx + dy], preferred_element_type=F32)
+            rhs = weights[9 * dx + 3 * dy : 9 * dx + 3 * dy + 3].reshape(768, 256)
+            part = jnp.dot(lhs, rhs, preferred_element_type=F32)
             acc = part if acc is None else acc + part
     return acc
 
@@ -130,17 +131,120 @@
 
 
 def kernel(
-    vol, fw, cw, fb, cb, out, recv, fine, coarse, done,
+    vol, fs, cs, fb, cb, out, recv, fine, coarse, done, fw, cw,
     in_send, in_recv, in_own, out_send, out_recv, out_own,
+    hop_send, hop_recv, twin_send, twin_recv, shard_own,
 ):
     me = lax.axis_index("space")
+    z = lax.axis_index("dp")
+    core = lax.rem(me, 2)
+    twin = me + 1 - 2 * core
+    shards, weights = (fs, cs), (fw, cw)
+    depth = fs.shape[1]
+    half = depth // 2
+    layers = 256 // depth
 
     barrier = pltpu.get_barrier_semaphore()
     for s in range(1, N):
         pl.semaphore_signal(
             barrier, inc=1, device_id={"space": lax.rem(me + s, N)}, device_id_type=MESH
         )
-    pl.semaphore_wait(barrier, N - 1)
+    for s in range(1, layers):
+        pl.semaphore_signal(
+            barrier, inc=1, device_id={"dp": lax.rem(z + s, layers)}, device_id_type=MESH
+        )
+    pl.semaphore_wait(barrier, N - 1 + layers - 1)
+
+    def rows(f, owner, which):
+        start = pl.multiple_of(owner * depth + which * half, half)
+        return weights[f].at[:, pl.ds(start, half)]
+
+    def valid(owner):
+        return (owner >= 0) & (owner < layers)
+
+    def hop(f, way, t):
+        sign = 1 - 2 * way
+        target = rows(f, z - sign * t, core)
+        source = target
+        if t == 0:
+            source = shards[f].at[:, pl.ds(pl.multiple_of(core * half, half), half)]
+        return pltpu.make_async_remote_copy(
+            src_ref=source,
+            dst_ref=target,
+            send_sem=hop_send.at[f, way, t],
+            recv_sem=hop_recv.at[f, way, t],
+            device_id={"dp": z + sign},
+            device_id_type=MESH,
+        )
+
+    def hop_landing(f, way, t):
+        sign = 1 - 2 * way
+        target = rows(f, z - sign * (t + 1), core)
+        return pltpu.make_async_remote_copy(
+            src_ref=target,
+            dst_ref=target,
+            send_sem=hop_send.at[f, way, t],
+            recv_sem=hop_recv.at[f, way, t],
+            device_id={"dp": z - sign},
+            device_id_type=MESH,
+        )
+
+    def pass_on(f, way, t, which):
+        sign = 1 - 2 * way
+        target = rows(f, z - sign * (t + 1), which)
+        return pltpu.make_async_remote_copy(
+            src_ref=target,
+            dst_ref=target,
+            send_sem=twin_send.at[f, way, t],
+            recv_sem=twin_recv.at[f, way, t],
+            device_id={"space": twin},
+            device_id_type=MESH,
+        )
+
+    def shard_copy(f):
+        start = pl.multiple_of(z * depth, depth)
+        return pltpu.make_async_copy(
+            shards[f], weights[f].at[:, pl.ds(start, depth)], shard_own.at[f]
+        )
+
+    def send_shard(f):
+        for way in range(2):
+            @pl.when(valid(z + 1 - 2 * way))
+            def _():
+                hop(f, way, 0).start()
+
+    def relay(f, t):
+        for way in range(2):
+            sign = 1 - 2 * way
+
+            @pl.when(valid(z - sign * (t + 1)))
+            def _():
+                hop_landing(f, way, t).wait_recv()
+                if t + 1 < layers - 1:
+                    @pl.when(valid(z + sign))
+                    def _():
+                        hop(f, way, t + 1).start()
+                pass_on(f, way, t, core).start()
+
+    def gathered(f):
+        shard_copy(f).wait()
+        for way in range(2):
+            for t in range(layers - 1):
+                @pl.when(valid(z - (1 - 2 * way) * (t + 1)))
+                def _():
+                    pass_on(f, way, t, 1 - core).wait_recv()
+
+    def all_sent(f):
+        for way in range(2):
+            sign = 1 - 2 * way
+            for t in range(layers - 1):
+                @pl.when(valid(z - sign * t) & valid(z + sign))
+                def _():
+                    hop(f, way, t).wait_send()
+
+                @pl.when(valid(z - sign * (t + 1)))
+                def _():
+                    pass_on(f, way, t, core).wait_send()
 
     def incoming(k, s):
         peer = lax.rem(me + s, N)
@@ -202,6 +306,7 @@
             device_id_type=MESH,
         )
 
+    send_shard(0)
     for k in range(2):
         incoming_own(k).start()
 
@@ -209,8 +314,14 @@
         def _(s):
             incoming(k, s).start()
 
+    shard_copy(0).start()
+    shard_copy(1).start()
     clear(fine, 1)
     clear(coarse, 2)
+    for t in range(layers - 1):
+        relay(0, t)
+        if t == layers - 3:
+            send_shard(1)
 
     @pl.loop(0, 2)
     def _(k):
@@ -227,12 +338,25 @@
             landing(k, s).wait_recv()
             take(lax.rem(me + N - s, N))
 
+        @pl.when(k == 0)
+        def _():
+            gathered(0)
+
         @pl.loop(0, S)
         def _(x):
+            for t in range(layers - 1):
+                @pl.when((k == 0) & (x == 5 + 5 * t))
+                def _():
+                    relay(1, t)
+
             total = taps(fine, x, 1, fw)
             own = fine[x + 1, pl.ds(1, S), :, 256:512].reshape(S * S, 256)
             middle = own.astype(F32) + jax.nn.gelu(total + fb[...])
             fill(coarse, x + 2, 2, middle.astype(jnp.bfloat16).reshape(S, S, 256), 8)
+
+        @pl.when(k == 0)
+        def _():
+            gathered(1)
 
         def finish(x):
             total = taps(coarse, x, 2, cw)
@@ -256,6 +380,8 @@
 
         outgoing_own(k).start()
 
+    all_sent(0)
+    all_sent(1)
     for k in range(2):
         outgoing_own(k).wait()
 
@@ -268,29 +394,34 @@
 
 def fused(volume, fine_filter, coarse_filter, fine_bias, coarse_bias):
     bf16 = jnp.bfloat16
-    fw = filters(fine_filter).reshape(9, 768, 256)
-    cw = filters(coarse_filter).reshape(9, 768, 256)
+    depth = fine_filter.shape[3]
+    layers = 256 // depth
     vmem = pl.BlockSpec(memory_space=pltpu.VMEM)
     hbm = pl.BlockSpec(memory_space=pl.ANY)
     dma = pltpu.SemaphoreType.DMA
     result = pl.pallas_call(
         kernel,
         out_shape=jax.ShapeDtypeStruct((2, 4, S, 4, S, 256), bf16),
-        in_specs=[hbm, vmem, vmem, vmem, vmem],
+        in_specs=[hbm, hbm, hbm, vmem, vmem],
         out_specs=hbm,
         scratch_shapes=[
             pltpu.VMEM((2, S, S, S, 256), bf16),
             pltpu.VMEM((S + 2, S + 2, S, 768), bf16),
             pltpu.VMEM((S + 4, S + 4, S, 768), bf16),
             pltpu.VMEM((2, S, S, S, 256), bf16),
+            pltpu.VMEM((27, 256, 256), bf16),
+            pltpu.VMEM((27, 256, 256), bf16),
             dma((2, N)), dma((2, N)), dma((2,)),
             dma((2, N)), dma((2, N)), dma((2,)),
+            dma((2, 2, layers - 1)), dma((2, 2, layers - 1)),
+            dma((2, 2, layers - 1)), dma((2, 2, layers - 1)), dma((2,)),
         ],
         compiler_params=pltpu.CompilerParams(
             collective_id=0, has_side_effects=True, vmem_limit_bytes=56 * 2**20
         ),
     )(
-        volume.reshape(2, 4, S, 4, S, 256), fw, cw,
+        volume.reshape(2, 4, S, 4, S, 256),
+        fine_filter.reshape(27, depth, 256), coarse_filter.reshape(27, depth, 256),
         fine_bias.reshape(1, 256), coarse_bias.reshape(1, 256),
     )
     return result.reshape(volume.shape)
@@ -298,7 +429,8 @@
 
 def on_device(volume, fine_filter, coarse_filter, fine_bias, coarse_bias):
     devices = lax.axis_size("space")
-    if devices == N and volume.shape == (1, 1, 8, 64, 16, 256):
+    fits = devices == N and lax.axis_size("dp") == 4
+    if fits and volume.shape == (1, 1, 8, 64, 16, 256):
         return fused(volume, fine_filter, coarse_filter, fine_bias, coarse_bias)
     brick = volume[0, 0]
     fine_weights = filters(fine_filter)

time: 277 us -> 141 us (0.51)
  waiting for transfers between devices: 144 us -> 0 us
  Pallas kernels: 116 us -> 136 us
  between operations: 13.4 us -> 0.01 us
    all_gather x2 -> x0, waiting for transfers between devices: 142 us -> none  [filters(): return lax.all_gather(shard, 'dp', axis=3, tiled=True)]
    pallas_call x1, Pallas kernels: 116 us -> 136 us  [fused(): pl.pallas_call(kernel, out_shape=jax.ShapeDtypeStruct((2, 4, S, 4, S, 256...]
  transfers between devices with their start and end apart: 2 -> 0, of which waited for: 2 -> 0; matrix products, arithmetic and copies ran while one was open for 0% -> 0% of each run, Pallas kernels for 0% -> 0%
where the time goes in v2:
time: 141 us
  Pallas kernels  136 us (96%)
  local copies, waits for them, and re-layouts  4.47 us (3%)
    pallas_call x1, Pallas kernels, fused(): pl.pallas_call(kernel, out_shape=jax.ShapeDtypeStruct((2, 4, S, 4, S, 256...  136 us
    unnamed x1, local copies, waits for them, and re-layouts  4.47 us

profile of v2, /device:TPU:3, one launch (start us, length us, event | category | flops | bytes accessed | tf_op | source)
XLA Modules:
  0.0 140.6 jit_solution(16116126375279560735)
XLA Ops:
  0.0 136.1 %shard_map.55 = bf16[2,4,16,4,16,256]{5,4,3,2,1,0:T(8,128)(2,1)} custom-call(bf16[2,4,16,4,16,256]{5,4,3,2,1,0:T(8,128)(2,1)} %bitcast.7, bf16[27,64,256]{2,1,0:T(8,128)(2,1)} %bitcast.8, bf16[27,64,256]{2,1,0:T(8,128)(2,1)} %bitcast.9, f32[1,256]{1,0:T(1,128)} %bitcast.10, f32[1,256]{1,0:T(1,128)} %bitcast.11), custom_call_target="tpu_custom_call" | custom-call | tf_op jit(solution)/shard_map/pallas_call | solution.py:402
  136.1 4.5 %copy.7 = bf16[1,1,8,64,16,256]{5,4,3,2,1,0:T(8,128)(2,1)} copy(bf16[1,1,8,64,16,256]{5,4,3,2,1,0:T(8,128)(2,1)} %bitcast.6) | data formatting | bytes 8388608
